TPU v7x, 256 devices: a whole 4x4x8 slice. The times are simulated.
256 devices in a mesh: sample: 2 (over z_hi), space: 8 (over y, core), filt: 16 (over z_lo, x).
Axes of the slice: x: 4, y: 4, z: 8 (z_hi: 2, z_lo: 4; z = z_hi * 4 + z_lo), core: 2. Of those that a mesh axis runs over, the one named last changes fastest.
Arguments:
- act_in: bfloat16 [2, 64, 16, 16, 128], P('sample', None, 'space'), may hold values from -6 to 6
- w_first: bfloat16 [27, 64, 128], P(None, None, 'filt'), may hold values from -0.15625 to 0.15625
- w_second: bfloat16 [27, 128, 128], P(None, None, 'filt'), may hold values from -0.109375 to 0.109375
- grad_out: bfloat16 [2, 128, 16, 16, 128], P('sample', 'filt', 'space'), may hold values from -6 to 6
Outputs:
- y_out: bfloat16 [2, 128, 16, 16, 128], P('sample', 'filt', 'space')
- grad_w_first: float32 [27, 64, 128], P(None, None, 'filt')
- grad_w_second: float32 [27, 128, 128], P(None, None, 'filt')
All inputs are finite; a program needn't handle non-finite values.
Results may differ from a plain program's by a relative error of at most 0.0054.
Values may be sent and summed in bfloat16 or wider, within the bound.
No kernel may reach another device: no remote copies, remote signals or barrier semaphores. Data moves between devices by JAX's collectives and lax.ppermute only.
A program may use at most 64 MiB of HBM per device.

v0:
```python
import math
import jax
import jax.numpy as jnp
from jax import lax
from jax.sharding import PartitionSpec as P


def padded(cells, sides, width):
    for axis, dim in sides:
        count = lax.axis_size(axis)
        ends = count - 1
        head = lax.slice_in_dim(cells, 0, width, axis=dim)
        tail = lax.slice_in_dim(cells, cells.shape[dim] - width, cells.shape[dim], axis=dim)
        cells = jnp.concatenate(
            [
                lax.ppermute(tail, axis, [(i, (i + 1) % count) for i in range(ends)]),
                cells,
                lax.ppermute(head, axis, [((i + 1) % count, i) for i in range(ends)]),
            ],
            axis=dim,
        )
    return cells


def correlate(source, kernel, rim_pad):
    taps = kernel.reshape(3, 3, 3, kernel.shape[1], kernel.shape[2])
    return lax.conv_general_dilated(
        source[None],
        taps,
        (1, 1, 1),
        ((0, 0), (rim_pad, rim_pad), (1, 1)),
        dimension_numbers=("NCDHW", "DHWIO", "NCDHW"),
        preferred_element_type=jnp.float32,
    )[0]


def transpose_correlate(gradient, kernel, rim_pad):
    taps = kernel.reshape(3, 3, 3, kernel.shape[1], kernel.shape[2])[::-1, ::-1, ::-1]
    return lax.conv_general_dilated(
        gradient[None],
        taps,
        (1, 1, 1),
        ((0, 0), (rim_pad, rim_pad), (1, 1)),
        dimension_numbers=("NCDHW", "DHWOI", "NCDHW"),
        preferred_element_type=jnp.float32,
    )[0]


def kernel_gradient(source, gradient, rim_pad):
    result = lax.conv_general_dilated(
        source[None],
        gradient[None],
        (1, 1, 1),
        ((0, 0), (rim_pad, rim_pad), (1, 1)),
        dimension_numbers=("CNDHW", "IODHW", "NCDHW"),
        preferred_element_type=jnp.float32,
    )
    return jnp.transpose(result, (2, 3, 4, 0, 1)).reshape(27, source.shape[0], gradient.shape[0])


def silu_slope(value):
    logistic = jax.nn.sigmoid(value)
    return logistic * (1.0 + value * (1.0 - logistic))


def local(act_in, w_first, w_second, grad_out):
    depth_rows = act_in.shape[2]
    height = act_in.shape[3]
    width = act_in.shape[4]
    n_space = lax.axis_size("space")
    n_sample = lax.axis_size("sample")
    slab = act_in[0]
    padded_in = padded(slab, (("space", 1),), 2)
    row_ids = lax.axis_index("space") * depth_rows - 1 + jnp.arange(depth_rows + 2, dtype=jnp.int32)
    inside = (row_ids >= 0) & (row_ids < depth_rows * n_space)
    z_first = correlate(padded_in, w_first, 1)
    act_ext = jnp.where(inside[None, :, None, None], jax.nn.silu(z_first), 0.0).astype(jnp.bfloat16)
    gathered = lax.all_gather(act_ext, "filt", axis=0, tiled=True)
    z_second = correlate(gathered, w_second, 1)
    y_local = jax.nn.silu(z_second).astype(jnp.bfloat16)
    grad_second = (grad_out[0].astype(jnp.float32) * silu_slope(z_second)).astype(jnp.bfloat16)
    grad_rim = padded(grad_second, (("space", 1),), 1)
    back_own = lax.psum_scatter(
        transpose_correlate(grad_rim, w_second, 1), "filt", scatter_dimension=0, tiled=True
    )
    dw_second = kernel_gradient(gathered, grad_second, 1)
    grad_first = (back_own * silu_slope(z_first[:, 1:-1])).astype(jnp.bfloat16)
    dw_first = kernel_gradient(padded_in[:, 1:-1], grad_first, 1)
    sum_first, sum_second = lax.psum((dw_first, dw_second), ("sample", "space"))
    factor = 1.0 / math.sqrt(n_sample * depth_rows * n_space * height * width)
    return (y_local[None], sum_first * factor, sum_second * factor)


def solution(mesh):
    placed = (
        P("sample", None, "space", None, None),
        P(None, None, "filt"),
        P(None, None, "filt"),
        P("sample", "filt", "space", None, None),
    )
    return jax.shard_map(
        local,
        mesh=mesh,
        in_specs=placed,
        out_specs=(
            P("sample", "filt", "space", None, None),
            P(None, None, "filt"),
            P(None, None, "filt"),
        ),
        check_vma=False,
    )
```

profile of v0, /device:TPU:0, one launch (start us, length us, event | category | flops | bytes accessed | tf_op | source)
XLA Modules:
  0.0 608.5 jit_solution(2420930683141478989)
XLA Ops:
  7.2 1.3 collective-permute-start
  8.6 1.3 collective-permute-start.1
  9.9 3.3 copy.90
  13.2 2.1 copy.93
  15.3 2.1 copy.94
  17.5 2.4 pad_maximum_fusion
  19.8 0.6 pad
  20.5 0.9 copy.96
  21.5 18.2 %broadcast_select_fusion = f32[4,16,8,17,8]{4,2,3,1,0:T(8,128)} fusion(pred[8,17]{0,1:T(8,128)(4,1)S(1)} %copy-done.5, bf16[3,3,3,64,8]{3,4,2,1,0:T(8,128)(2,1)S(1)} %bitcast.98, bf16[64,6,16,1,7,2]{0,4,5,2,1,3:T(8,128)(2,1)S(1)} %slice.24, bf16[64,6,16,1,8,17]{0,4,5,2,1,3:T(8,128)(2,1)S(1)} %copy.96), kind=kOutput, calls=%fused_computation.27 | convolution fusion | flops 236294144 | bytes 2149512 | tf_op jit(solution)/shard_map/conv_general_dilated | solution.py:27
  39.6 6.1 %copy.97 = f32[4,16,8,17,8]{3,2,4,1,0:T(8,128)} copy(f32[4,16,8,17,8]{4,2,3,1,0:T(8,128)} %broadcast_select_fusion) | data formatting | bytes 557056 | tf_op jit(solution)/shard_map/conv_general_dilated | solution.py:27
  45.8 2.8 reshape.38
  48.5 1.7 select_convert_fusion
  50.3 80.8 %all-gather.2.cloned.1.call-done = bf16[128,4,16,128]{3,0,2,1:T(8,128)(2,1)} async-done(((bf16[8,4,16,128]{3,0,2,1:T(8,128)(2,1)}), bf16[128,4,16,128]{3,0,2,1:T(8,128)(2,1)}) %all-gather.2.cloned.1.call-update) | async-done | bytes 2097168 | tf_op jit(solution)/shard_map/all_gather | solution.py:78
  131.1 4.9 copy.127
  136.0 2.0 pad.2.clone
  137.9 0.6 copy.100
  138.6 9.6 %fusion.18 = f32[2,16,8,17,8]{4,2,3,1,0:T(8,128)} fusion(bf16[3,3,3,128,8]{3,4,2,1,0:T(8,128)(2,1)S(1)} %bitcast.85, bf16[128,4,16,1,7,2]{0,4,5,2,1,3:T(8,128)(2,1)S(1)} %slice.26, bf16[128,4,16,1,8,17]{0,4,5,2,1,3:T(8,128)(2,1)S(1)} %copy.100), kind=kOutput, calls=%fused_computation.20 | convolution fusion | flops 238092288 | bytes 2652160 | tf_op jit(solution)/shard_map/conv_general_dilated | solution.py:27
  148.3 3.7 copy.101
  151.9 2.9 add_multiply_fusion
  154.8 1.2 copy.115
  155.9 1.5 reshape.56
  157.5 2.4 copy.106
  159.9 2.2 reshape.45
  162.1 0.9 fusion.36
  163.0 1.0 fusion.35
  164.0 1.3 collective-permute-start.2
  165.3 1.3 collective-permute-start.3
  166.6 3.7 copy.117
  170.3 10.7 %copy.116 = bf16[1,128,4,16,128]{1,0,4,3,2:T(2,128)(2,1)} copy(bf16[1,128,4,16,128]{4,1,3,2,0:T(8,128)(2,1)} %bitcast.91) | data formatting | bytes 4194304 | tf_op jit(solution)/shard_map/broadcast_in_dim | solution.py:28
  181.0 31.9 %fusion.49 = f32[3,3,3,128,8]{3,4,2,1,0:T(8,128)} fusion(bf16[1,128,4,16,128]{1,0,4,3,2:T(2,128)(2,1)} %copy.116, bf16[1,8,2,16,128]{1,0,4,3,2:T(2,128)(2,1)} %copy.117), kind=kOutput, calls=%fused_computation.64 | convolution fusion | flops 215924736 | bytes 2273280 | tf_op jit(solution)/shard_map/transpose | solution.py:58
  213.2 1.7 reshape.75
  214.9 5.6 copy.109
  220.5 1.0 slice.32
  221.5 5.2 fusion.29
  226.7 0.4 copy.110
  227.2 1.4 slice.33
  228.6 3.0 copy.126
  231.6 1.0 slice_bitcast_fusion.1
  232.7 1.7 slice_bitcast_fusion
  234.8 0.6 copy.118
  235.4 152.0 %all-reduce.2.cloned.1.call-done = f32[27,128,8]{1,2,0:T(8,128)} async-done(((f32[27,128,8]{1,2,0:T(8,128)}), f32[27,128,8]{1,2,0:T(8,128)}) %all-reduce.2.cloned.1.call-update) | async-done | bytes 110608 | tf_op jit(solution)/shard_map/psum | solution.py:89
  387.5 1.5 broadcast_multiply_fusion
  389.0 88.9 %reduce-scatter.2.cloned.1.call-done = f32[8,2,16,128]{3,0,2,1:T(8,128)} async-done(((f32[128,2,16,128]{3,0,2,1:T(8,128)}), f32[8,2,16,128]{3,0,2,1:T(8,128)}) %reduce-scatter.2.cloned.1.call-update) | async-done | bytes 131088 | tf_op jit(solution)/shard_map/reduce_scatter | solution.py:83
  477.9 1.0 fusion.37
  478.8 3.7 copy.113
  482.6 33.6 %fusion.3 = f32[3,3,3,64,8]{3,4,2,1,0:T(8,128)S(1)} fusion(bf16[1,8,2,16,128]{1,0,4,3,2:T(2,128)(2,1)} %copy.113, bf16[1,64,4,16,128]{1,3,4,2,0:T(8,128)(2,1)S(1)} %copy-done.1), kind=kOutput, calls=%fused_computation.6 | convolution fusion | flops 107962368 | bytes 1169408 | tf_op jit(solution)/shard_map/transpose | solution.py:58
  516.2 85.0 %psum.14 = f32[27,64,8]{1,2,0:T(8,128)S(1)} all-reduce(f32[27,64,8]{1,2,0:T(8,128)S(1)} %bitcast.97), channel_id=1, replica_groups=mesh['sample'=2,'space'=8,'filt'=16] {'sample','space'}, use_global_device_ids=true, to_apply=%region_1.2 | all-reduce | flops 13824 | bytes 110592 | tf_op jit(solution)/shard_map/psum | solution.py:89
  601.1 0.7 broadcast_multiply_fusion.1
  (31 shorter events, 1.0 us)
Async XLA Ops:
  7.2 131.4 %copy-start = (bf16[27,128,8]{1,2,0:T(8,128)(2,1)S(1)}, bf16[27,128,8]{1,2,0:T(8,128)(2,1)}, u32[]{:S(2)}) copy-start(bf16[27,128,8]{1,2,0:T(8,128)(2,1)} %param.6) | copy-start | bytes 165892
  7.2 123.9 %all-gather.2.cloned.1.call-start = ((), (), s32[]{:S(2)}) async-start(), calls=%async_computation.1 | async-start | bytes 2228224 | tf_op jit(solution)/shard_map/all_gather | solution.py:78
  7.2 5.9 collective-permute-start
  8.6 6.8 %collective-permute-start.1 = (bf16[64,2,16,128]{3,2,1,0:T(8,128)(2,1)}, bf16[64,2,16,128]{3,2,1,0:T(8,128)(2,1)S(1)}, u32[]{:S(2)}, u32[]{:S(2)}) collective-permute-start(bf16[64,2,16,128]{3,2,1,0:T(8,128)(2,1)} %bitcast.95), channel_id=1, source_target_pairs={{16,0},{32,16},{48,32},{64,48},{80,64},{96,80},{112,96},{17,1},{33... | collective-permute-start | bytes 1572872 | tf_op jit(solution)/shard_map/ppermute | solution.py:18
  20.5 1.0 copy-start.4
  20.5 1.0 copy-start.5
  50.3 337.2 %all-reduce.2.cloned.1.call-start = ((), (), s32[]{:S(2)}) async-start(), calls=%async_computation.3 | async-start | bytes 221184 | tf_op jit(solution)/shard_map/psum | solution.py:89
  148.3 3.7 copy-start.3
  164.0 49.0 %collective-permute-start.2 = (bf16[8,1,16,128]{3,0,2,1:T(8,128)(2,1)S(1)}, bf16[8,1,16,128]{3,0,2,1:T(8,128)(2,1)S(1)}, u32[]{:S(2)}, u32[]{:S(2)}) collective-permute-start(bf16[8,1,16,128]{3,0,2,1:T(8,128)(2,1)S(1)} %get-tuple-element.20), channel_id=1, source_target_pairs={{0,16},{16,32},{32,48},{48,64},{64,80},{80,96},{96,112},{1,17},{17... | collective-permute-start | bytes 98312 | tf_op jit(solution)/shard_map/ppermute | solution.py:16
  165.3 47.7 %collective-permute-start.3 = (bf16[8,1,16,128]{3,0,2,1:T(8,128)(2,1)S(1)}, bf16[8,1,16,128]{3,0,2,1:T(8,128)(2,1)S(1)}, u32[]{:S(2)}, u32[]{:S(2)}) collective-permute-start(bf16[8,1,16,128]{3,0,2,1:T(8,128)(2,1)S(1)} %get-tuple-element.21), channel_id=1, source_target_pairs={{16,0},{32,16},{48,32},{64,48},{80,64},{96,80},{112,96},{17,1},{33... | collective-permute-start | bytes 98312 | tf_op jit(solution)/shard_map/ppermute | solution.py:18
  212.9 264.9 %reduce-scatter.2.cloned.1.call-start = ((), (), s32[]{:S(2)}) async-start(), calls=%async_computation.2 | async-start | bytes 2228224 | tf_op jit(solution)/shard_map/reduce_scatter | solution.py:83
  231.6 2.7 copy-start.2
  234.3 248.2 %copy-start.1 = (bf16[1,64,4,16,128]{1,3,4,2,0:T(8,128)(2,1)S(1)}, bf16[1,64,4,16,128]{1,3,4,2,0:T(8,128)(2,1)}, u32[]{:S(2)}) copy-start(bf16[1,64,4,16,128]{1,3,4,2,0:T(8,128)(2,1)} %slice_bitcast_fusion) | copy-start | bytes 3145732
Sparse Core Ops, SparseCore 0:
  50.4 80.6 all-gather.1
  213.1 174.3 all-reduce.1
  390.2 87.6 reduce-scatter.1
where the time goes:
time: 613 us; the launch traced here: 609 us
  waiting for transfers between devices  322 us (53%)
  matrix products  98.5 us (16%)
  blocking collectives  85 us (14%)
  local copies, waits for them, and re-layouts  71.8 us (12%)
  between operations  14.2 us (2%)
  other arithmetic  11.9 us (2%)
    psum x1, waiting for transfers between devices, local(): sum_first, sum_second = lax.psum((dw_first, dw_second), ('sample', 'space'))  152 us
    reduce_scatter x1, waiting for transfers between devices, local(): lax.psum_scatter(transpose_correlate(grad_rim, w_second, 1), 'filt', scat...  88.9 us
    psum x1, blocking collectives, local(): sum_first, sum_second = lax.psum((dw_first, dw_second), ('sample', 'space'))  85 us
    all_gather x1, waiting for transfers between devices, local(): gathered = lax.all_gather(act_ext, 'filt', axis=0, tiled=True)  80.8 us
    transpose x2, matrix products, kernel_gradient(): jnp.transpose(result, (2, 3, 4, 0, 1))  65.5 us
    conv_general_dilated x2, matrix products, correlate(): lax.conv_general_dilated(source[None], taps, (1, 1, 1), ((0, 0), (rim_pad...  27.8 us
    conv_general_dilated x9, local copies, waits for them, and re-layouts, correlate(): lax.conv_general_dilated(source[None], taps, (1, 1, 1), ((0, 0), (rim_pad...  18.8 us
    broadcast_in_dim x3, local copies, waits for them, and re-layouts, correlate(): source[None]  13.3 us
  transfers between devices with their start and end apart: 7, of which 3 were waited for; matrix products, arithmetic and copies ran while one was open for 12% of the time, Pallas kernels for 0%

commit v1 on v0

--- a/solution.py
+++ b/solution.py
@@ -3,6 +3,11 @@
 import jax.numpy as jnp
 from jax import lax
 from jax.sharding import PartitionSpec as P
+
+
+def axis_by_axis(array, one, other):
+    partial = lax.psum(array, one)
+    return lax.psum(partial, other)
 
 
 def padded(cells, sides, width):
@@ -86,7 +91,7 @@
     dw_second = kernel_gradient(gathered, grad_second, 1)
     grad_first = (back_own * silu_slope(z_first[:, 1:-1])).astype(jnp.bfloat16)
     dw_first = kernel_gradient(padded_in[:, 1:-1], grad_first, 1)
-    sum_first, sum_second = lax.psum((dw_first, dw_second), ("sample", "space"))
+    sum_first, sum_second = axis_by_axis((dw_first, dw_second), "sample", "space")
     factor = 1.0 / math.sqrt(n_sample * depth_rows * n_space * height * width)
     return (y_local[None], sum_first * factor, sum_second * factor)
 

time: 613 us -> 496 us (0.81)
  waiting for transfers between devices: 322 us -> 250 us
  blocking collectives: 85 us -> 39.2 us
    psum x1 -> x2, waiting for transfers between devices: 152 us -> 79.8 us  [the longest x1 47.7 us: axis_by_axis(): return lax.psum(partial, other)]
    psum x1 -> x2, blocking collectives: 85 us -> 39.2 us  [the longest x1 24.8 us: axis_by_axis(): return lax.psum(partial, other)]
  transfers between devices with their start and end apart: 7 -> 8, of which waited for: 3 -> 4; matrix products, arithmetic and copies ran while one was open for 12% -> 15% of each run, Pallas kernels for 0% -> 0%
where the time goes in v1:
time: 496 us; the launch traced here: 491 us
  waiting for transfers between devices  250 us (50%)
  matrix products  98.5 us (20%)
  local copies, waits for them, and re-layouts  72 us (15%)
  blocking collectives  39.2 us (8%)
  between operations  14.3 us (3%)
  other arithmetic  11.9 us (2%)
  starting transfers between devices  5.36 us (1%)
    reduce_scatter x1, waiting for transfers between devices, local(): lax.psum_scatter(transpose_correlate(grad_rim, w_second, 1), 'filt', scat...  89 us
    all_gather x1, waiting for transfers between devices, local(): gathered = lax.all_gather(act_ext, 'filt', axis=0, tiled=True)  80.7 us
    transpose x2, matrix products, kernel_gradient(): jnp.transpose(result, (2, 3, 4, 0, 1))  65.5 us
    psum x1, waiting for transfers between devices, axis_by_axis(): return lax.psum(partial, other)  47.7 us
    psum x1, waiting for transfers between devices, axis_by_axis(): partial = lax.psum(array, one)  32.1 us
    conv_general_dilated x2, matrix products, correlate(): lax.conv_general_dilated(source[None], taps, (1, 1, 1), ((0, 0), (rim_pad...  27.8 us
    psum x1, blocking collectives, axis_by_axis(): return lax.psum(partial, other)  24.8 us
    conv_general_dilated x9, local copies, waits for them, and re-layouts, correlate(): lax.conv_general_dilated(source[None], taps, (1, 1, 1), ((0, 0), (rim_pad...  18.9 us
  transfers between devices with their start and end apart: 8, of which 4 were waited for; matrix products, arithmetic and copies ran while one was open for 15% of the time, Pallas kernels for 0%

profile of v1, /device:TPU:0, one launch (start us, length us, event | category | flops | bytes accessed | tf_op | source)
XLA Modules:
  0.0 490.9 jit_solution(11725215078133851265)
XLA Ops:
  7.2 1.3 collective-permute-start
  8.6 1.3 collective-permute-start.1
  9.9 3.3 copy.90
  13.2 2.2 copy.93
  15.3 2.1 copy.94
  17.5 2.4 pad_maximum_fusion
  19.9 0.6 pad
  20.5 0.9 copy.96
  21.5 18.1 %broadcast_select_fusion = f32[4,16,8,17,8]{4,2,3,1,0:T(8,128)} fusion(pred[8,17]{0,1:T(8,128)(4,1)S(1)} %copy-done.5, bf16[3,3,3,64,8]{3,4,2,1,0:T(8,128)(2,1)S(1)} %bitcast.98, bf16[64,6,16,1,7,2]{0,4,5,2,1,3:T(8,128)(2,1)S(1)} %slice.24, bf16[64,6,16,1,8,17]{0,4,5,2,1,3:T(8,128)(2,1)S(1)} %copy.96), kind=kOutput, calls=%fused_computation.27 | convolution fusion | flops 236294144 | bytes 2149512 | tf_op jit(solution)/shard_map/conv_general_dilated | solution.py:32
  39.7 6.2 %copy.97 = f32[4,16,8,17,8]{3,2,4,1,0:T(8,128)} copy(f32[4,16,8,17,8]{4,2,3,1,0:T(8,128)} %broadcast_select_fusion) | data formatting | bytes 557056 | tf_op jit(solution)/shard_map/conv_general_dilated | solution.py:32
  45.8 2.8 reshape.38
  48.6 1.7 select_convert_fusion
  50.4 80.7 %all-gather.2.cloned.1.call-done = bf16[128,4,16,128]{3,0,2,1:T(8,128)(2,1)} async-done(((bf16[8,4,16,128]{3,0,2,1:T(8,128)(2,1)}), bf16[128,4,16,128]{3,0,2,1:T(8,128)(2,1)}) %all-gather.2.cloned.1.call-update) | async-done | bytes 2097168 | tf_op jit(solution)/shard_map/all_gather | solution.py:83
  131.1 4.9 copy.127
  136.0 2.0 pad.2.clone
  138.6 9.6 %fusion.18 = f32[2,16,8,17,8]{4,2,3,1,0:T(8,128)} fusion(bf16[3,3,3,128,8]{3,4,2,1,0:T(8,128)(2,1)S(1)} %bitcast.85, bf16[128,4,16,1,7,2]{0,4,5,2,1,3:T(8,128)(2,1)S(1)} %slice.26, bf16[128,4,16,1,8,17]{0,4,5,2,1,3:T(8,128)(2,1)S(1)} %copy.100), kind=kOutput, calls=%fused_computation.20 | convolution fusion | flops 238092288 | bytes 2652160 | tf_op jit(solution)/shard_map/conv_general_dilated | solution.py:32
  148.3 3.7 copy.101
  152.0 2.8 add_multiply_fusion
  154.8 1.2 copy.115
  156.0 1.5 reshape.56
  157.5 2.4 copy.106
  159.9 2.2 reshape.45
  162.1 0.9 fusion.36
  163.0 1.0 fusion.35
  164.0 1.3 collective-permute-start.2
  165.3 1.3 collective-permute-start.3
  166.6 3.7 copy.117
  170.3 10.7 %copy.116 = bf16[1,128,4,16,128]{1,0,4,3,2:T(2,128)(2,1)} copy(bf16[1,128,4,16,128]{4,1,3,2,0:T(8,128)(2,1)} %bitcast.91) | data formatting | bytes 4194304 | tf_op jit(solution)/shard_map/broadcast_in_dim | solution.py:33
  181.1 31.9 %fusion.49 = f32[3,3,3,128,8]{3,4,2,1,0:T(8,128)} fusion(bf16[1,128,4,16,128]{1,0,4,3,2:T(2,128)(2,1)} %copy.116, bf16[1,8,2,16,128]{1,0,4,3,2:T(2,128)(2,1)} %copy.117), kind=kOutput, calls=%fused_computation.64 | convolution fusion | flops 215924736 | bytes 2273280 | tf_op jit(solution)/shard_map/transpose | solution.py:63
  213.3 1.7 reshape.75
  215.0 5.6 %copy.109 = bf16[8,4,16,1,8,17]{0,4,5,2,1,3:T(8,128)(2,1)} copy(bf16[8,4,16,1,8,17]{5,4,0,2,1,3:T(8,128)(2,1)} %reshape.75) | data formatting | bytes 278528 | tf_op jit(solution)/shard_map/conv_general_dilated | solution.py:44
  220.6 1.0 slice.32
  221.6 32.1 %all-reduce.3.cloned.1.call-done = f32[27,128,8]{1,2,0:T(8,128)} async-done(((f32[27,128,8]{1,2,0:T(8,128)}), f32[27,128,8]{1,2,0:T(8,128)}) %all-reduce.3.cloned.1.call-update) | async-done | bytes 110608 | tf_op jit(solution)/shard_map/psum | solution.py:9
  253.8 5.2 %fusion.29 = f32[2,16,8,17,128]{4,2,3,1,0:T(8,128)S(1)} fusion(bf16[3,3,3,128,8]{3,4,2,1,0:T(8,128)(2,1)S(1)} %bitcast.86, bf16[8,4,16,1,7,2]{0,4,5,2,1,3:T(8,128)(2,1)S(1)} %slice.32, bf16[8,4,16,1,8,17]{0,4,5,2,1,3:T(8,128)(2,1)} %copy.109, pred[8,17]{0,1:T(8,128)(4,1)S(1)} %copy-done.5), kind=kOutput, calls=%fused_computation.30 | convolution fusion | flops 231645184 | bytes 2437256 | tf_op jit(solution)/shard_map/conv_general_dilated | solution.py:44
  259.4 1.5 slice.33
  260.9 3.0 copy.126
  263.9 1.0 slice_bitcast_fusion.1
  265.0 1.7 slice_bitcast_fusion
  267.1 0.6 copy.118
  267.7 47.7 %all-reduce.5.cloned.1.call-done = f32[27,128,8]{1,2,0:T(8,128)} async-done(((f32[27,128,8]{1,2,0:T(8,128)}), f32[27,128,8]{1,2,0:T(8,128)}) %all-reduce.5.cloned.1.call-update) | async-done | bytes 110608 | tf_op jit(solution)/shard_map/psum | solution.py:10
  315.4 1.5 broadcast_multiply_fusion
  317.0 89.0 %reduce-scatter.2.cloned.1.call-done = f32[8,2,16,128]{3,0,2,1:T(8,128)} async-done(((f32[128,2,16,128]{3,0,2,1:T(8,128)}), f32[8,2,16,128]{3,0,2,1:T(8,128)}) %reduce-scatter.2.cloned.1.call-update) | async-done | bytes 131088 | tf_op jit(solution)/shard_map/reduce_scatter | solution.py:88
  406.0 1.0 fusion.37
  407.0 3.7 copy.113
  410.7 33.6 %fusion.3 = f32[3,3,3,64,8]{3,4,2,1,0:T(8,128)S(1)} fusion(bf16[1,8,2,16,128]{1,0,4,3,2:T(2,128)(2,1)} %copy.113, bf16[1,64,4,16,128]{1,3,4,2,0:T(8,128)(2,1)S(1)} %copy-done.1), kind=kOutput, calls=%fused_computation.6 | convolution fusion | flops 107962368 | bytes 1169408 | tf_op jit(solution)/shard_map/transpose | solution.py:63
  444.3 14.4 %psum.28 = f32[27,64,8]{1,2,0:T(8,128)S(1)} all-reduce(f32[27,64,8]{1,2,0:T(8,128)S(1)} %bitcast.97), channel_id=1, replica_groups=mesh['sample'=2,'space'=8,'filt'=16] {'sample'}, use_global_device_ids=true, to_apply=%region_1.2 | all-reduce | flops 13824 | bytes 110592 | tf_op jit(solution)/shard_map/psum | solution.py:9
  458.7 24.8 %psum.29 = f32[27,64,8]{1,2,0:T(8,128)S(1)} all-reduce(f32[27,64,8]{1,2,0:T(8,128)S(1)} %psum.28), channel_id=1, replica_groups=mesh['sample'=2,'space'=8,'filt'=16] {'space'}, use_global_device_ids=true, to_apply=%region_2.3 | all-reduce | flops 13824 | bytes 110592 | tf_op jit(solution)/shard_map/psum | solution.py:10
  483.5 0.7 broadcast_multiply_fusion.1
  (35 shorter events, 2.1 us)
Async XLA Ops:
  7.2 131.5 %copy-start = (bf16[27,128,8]{1,2,0:T(8,128)(2,1)S(1)}, bf16[27,128,8]{1,2,0:T(8,128)(2,1)}, u32[]{:S(2)}) copy-start(bf16[27,128,8]{1,2,0:T(8,128)(2,1)} %param.6) | copy-start | bytes 165892
  7.2 123.9 %all-gather.2.cloned.1.call-start = ((), (), s32[]{:S(2)}) async-start(), calls=%async_computation.1 | async-start | bytes 2228224 | tf_op jit(solution)/shard_map/all_gather | solution.py:83
  7.2 6.0 %collective-permute-start = (bf16[64,2,16,128]{3,2,1,0:T(8,128)(2,1)}, bf16[64,2,16,128]{3,2,1,0:T(8,128)(2,1)S(1)}, u32[]{:S(2)}, u32[]{:S(2)}) collective-permute-start(bf16[64,2,16,128]{3,2,1,0:T(8,128)(2,1)} %bitcast.94), channel_id=1, source_target_pairs={{0,16},{16,32},{32,48},{48,64},{64,80},{80,96},{96,112},{1,17},{17... | collective-permute-start | bytes 1572872 | tf_op jit(solution)/shard_map/ppermute | solution.py:21
  8.6 6.8 %collective-permute-start.1 = (bf16[64,2,16,128]{3,2,1,0:T(8,128)(2,1)}, bf16[64,2,16,128]{3,2,1,0:T(8,128)(2,1)S(1)}, u32[]{:S(2)}, u32[]{:S(2)}) collective-permute-start(bf16[64,2,16,128]{3,2,1,0:T(8,128)(2,1)} %bitcast.95), channel_id=1, source_target_pairs={{16,0},{32,16},{48,32},{64,48},{80,64},{96,80},{112,96},{17,1},{33... | collective-permute-start | bytes 1572872 | tf_op jit(solution)/shard_map/ppermute | solution.py:23
  20.5 1.0 copy-start.4
  20.5 1.0 copy-start.5
  50.3 203.4 %all-reduce.3.cloned.1.call-start = ((), (), s32[]{:S(2)}) async-start(), calls=%async_computation.3 | async-start | bytes 221184 | tf_op jit(solution)/shard_map/psum | solution.py:9
  148.3 3.7 copy-start.3
  164.0 49.1 %collective-permute-start.2 = (bf16[8,1,16,128]{3,0,2,1:T(8,128)(2,1)S(1)}, bf16[8,1,16,128]{3,0,2,1:T(8,128)(2,1)S(1)}, u32[]{:S(2)}, u32[]{:S(2)}) collective-permute-start(bf16[8,1,16,128]{3,0,2,1:T(8,128)(2,1)S(1)} %get-tuple-element.20), channel_id=1, source_target_pairs={{0,16},{16,32},{32,48},{48,64},{64,80},{80,96},{96,112},{1,17},{17... | collective-permute-start | bytes 98312 | tf_op jit(solution)/shard_map/ppermute | solution.py:21
  165.3 47.8 %collective-permute-start.3 = (bf16[8,1,16,128]{3,0,2,1:T(8,128)(2,1)S(1)}, bf16[8,1,16,128]{3,0,2,1:T(8,128)(2,1)S(1)}, u32[]{:S(2)}, u32[]{:S(2)}) collective-permute-start(bf16[8,1,16,128]{3,0,2,1:T(8,128)(2,1)S(1)} %get-tuple-element.21), channel_id=1, source_target_pairs={{16,0},{32,16},{48,32},{64,48},{80,64},{96,80},{112,96},{17,1},{33... | collective-permute-start | bytes 98312 | tf_op jit(solution)/shard_map/ppermute | solution.py:23
  213.0 102.4 %all-reduce.5.cloned.1.call-start = ((), (), s32[]{:S(2)}) async-start(), calls=%async_computation.4 | async-start | bytes 221184 | tf_op jit(solution)/shard_map/psum | solution.py:10
  253.7 152.3 %reduce-scatter.2.cloned.1.call-start = ((), (), s32[]{:S(2)}) async-start(), calls=%async_computation.2 | async-start | bytes 2228224 | tf_op jit(solution)/shard_map/reduce_scatter | solution.py:88
  263.9 2.7 copy-start.2
  266.6 144.1 %copy-start.1 = (bf16[1,64,4,16,128]{1,3,4,2,0:T(8,128)(2,1)S(1)}, bf16[1,64,4,16,128]{1,3,4,2,0:T(8,128)(2,1)}, u32[]{:S(2)}) copy-start(bf16[1,64,4,16,128]{1,3,4,2,0:T(8,128)(2,1)} %slice_bitcast_fusion) | copy-start | bytes 3145732
Sparse Core Ops, SparseCore 0:
  50.5 80.6 all-gather.1
  213.1 40.5 all-reduce.2
  256.0 59.3 all-reduce.4
  318.0 87.9 reduce-scatter.1
